TPU v7x, 256 devices: a whole 4x4x8 slice. The times are simulated.
256 devices in a mesh: dp: 4 (over x), ctx: 64 (over z, y, core).
Axes of the slice: x: 4, y: 4, z: 8, core: 2. Of those that a mesh axis runs over, the one named last changes fastest.
Arguments:
- query_in: bfloat16 [4, 16384, 2048], P('dp', 'ctx'), may hold values from -68 to 68
- key_in: bfloat16 [4, 16384, 2048], P('dp', 'ctx'), may hold values from -6 to 6
- value_in: bfloat16 [4, 16384, 2048], P('dp', 'ctx'), may hold values from -6 to 6
- conv_weight: float32 [3, 4, 2048], replicated, may hold values from -3 to 3
- out_grad: bfloat16 [4, 16384, 2048], P('dp', 'ctx'), may hold values from -6 to 6
- block_lists: int32 [4, 256, 16], P('dp', 'ctx'), may hold values from 0 to 255, as said below
Outputs:
- query_in_grad: bfloat16 [4, 16384, 2048], P('dp', 'ctx')
- key_in_grad: bfloat16 [4, 16384, 2048], P('dp', 'ctx')
- value_in_grad: bfloat16 [4, 16384, 2048], P('dp', 'ctx')
- conv_grad: float32 [3, 4, 2048], replicated
Inputs may be any that keep to these rules, and one draw needn't show every extreme that they name: `block_lists`: entry n names key block n of the sequence. Each list names the 1 key block of its own query block and no block twice. The lists in the rows of ctx index i name only blocks held by ctx index i or by ctx indices (i - d) mod 64 for d = 1 to 6, and at most 2 distinct blocks held by any one other index; this most is reached.
All inputs are finite; a program needn't handle non-finite values.
Results may differ from a plain program's by a relative error of at most 0.012.
The roundings to bfloat16 on the way count: a program that leaves them out, or rounds other values in their place, can miss the bound.
Values may be sent and summed in bfloat16 or wider, within the bound.
No kernel may reach another device: no remote copies, remote signals or barrier semaphores. Data moves between devices by JAX's collectives and lax.ppermute only.
A program may use at most 192 MiB of HBM per device.

v0:
```python
import math

import jax
import jax.numpy as jnp
from jax import lax
from jax.sharding import PartitionSpec as P

HEAD = 128
TAPS = 4
QBLK = 64
KBLK = 64
DEVICES_BEHIND = 6
MAX_REMOTE_KEYS = 2


def with_halo(x, sides, width):
    for axis, dim in sides:
        count, length = (lax.axis_size(axis), x.shape[dim])
        up = [(i, (i + 1) % count) for i in range(count - 1)]
        down = [(j, i) for i, j in up]
        last = lax.slice_in_dim(x, length - width, length, axis=dim)
        leading = lax.slice_in_dim(x, 0, width, axis=dim)
        before = lax.ppermute(last, axis, up)
        after = lax.ppermute(leading, axis, down)
        x = jnp.concatenate([before, x, after], axis=dim)
    return x


def passed_along(x, axis, by):
    count = lax.axis_size(axis)
    return lax.ppermute(x, axis, [(i, (i + by) % count) for i in range(count)])


def for_sending(x):
    return jax.tree.map(lambda a: a.astype(jnp.bfloat16) if a.dtype == jnp.float32 else a, x)


def locate(lists, half_rows, group_width):
    span_index = lists * KBLK // half_rows
    upper_mask = span_index >= group_width
    owners = jnp.where(upper_mask, 2 * group_width - 1 - span_index, span_index)
    local_index = (
        jnp.where(upper_mask, half_rows // KBLK, 0)
        + (lists * KBLK - span_index * half_rows) // KBLK
    )
    return (owners, local_index)


def pick_slots(wanted, slot_cap):
    slot_rank = jnp.cumsum(wanted.astype(jnp.int32), axis=1) - 1
    block_ids = jnp.arange(wanted.shape[1], dtype=jnp.int32)
    hits = wanted[:, :, None] & (
        slot_rank[:, :, None] == jnp.arange(slot_cap, dtype=jnp.int32)[None, None, :]
    )
    chosen = jnp.sum(jnp.where(hits, block_ids[None, :, None], 0), axis=1)
    return (jnp.where(jnp.any(hits, axis=1), chosen, -1), slot_rank)


def convolve(extended, weight, length):
    rim_rows = TAPS - 1
    result = weight[:, 0, None, :] * extended[:, rim_rows : rim_rows + length]
    for offset in range(1, TAPS):
        result = (
            result
            + weight[:, offset, None, :]
            * extended[:, rim_rows - offset : rim_rows - offset + length]
        )
    return result


def unconvolve(extended, weight, length):
    result = weight[:, 0, None, :] * extended[:, :length]
    for offset in range(1, TAPS):
        result = result + weight[:, offset, None, :] * extended[:, offset : offset + length]
    return result


def tap_sums(grad_rows, extended):
    length = grad_rows.shape[1]
    rim_rows = TAPS - 1
    return jnp.stack(
        [
            jnp.sum(grad_rows * extended[:, rim_rows - offset : rim_rows - offset + length], axis=1)
            for offset in range(TAPS)
        ],
        axis=1,
    )


def body(query_in, key_in, value_in, conv_weight, out_grad, block_lists):
    stacked = jnp.stack([query_in[0], key_in[0], value_in[0]])
    tok_rows = stacked.shape[1]
    half_rows = tok_rows // 2
    channels = stacked.shape[2]
    rim_rows = TAPS - 1
    group_width = lax.axis_size("ctx")
    my_index = lax.axis_index("ctx")
    is_last = my_index == group_width - 1
    edge_rows = jnp.concatenate(
        [stacked[:, tok_rows - rim_rows :], stacked[:, half_rows - rim_rows : half_rows]], axis=1
    )
    edged = with_halo(edge_rows, (("ctx", 1),), rim_rows)
    before_low = edged[:, :rim_rows]
    before_high = jnp.where(
        is_last, stacked[:, half_rows - rim_rows : half_rows], edged[:, 3 * rim_rows :]
    )
    extended_low = jnp.concatenate([before_low, stacked[:, :half_rows]], axis=1).astype(jnp.float32)
    extended_high = jnp.concatenate([before_high, stacked[:, half_rows:]], axis=1).astype(
        jnp.float32
    )
    fields = jnp.concatenate(
        [
            convolve(extended_low, conv_weight, half_rows),
            convolve(extended_high, conv_weight, half_rows),
        ],
        axis=1,
    ).astype(jnp.bfloat16)
    spread = jnp.arange(half_rows, dtype=jnp.int32)
    positions = jnp.concatenate(
        [my_index * half_rows + spread, (2 * group_width - 1 - my_index) * half_rows + spread]
    )
    lists = block_lists[0]
    key_blocks = tok_rows // KBLK
    remote_slots = DEVICES_BEHIND * MAX_REMOTE_KEYS
    slots_total = remote_slots + key_blocks
    block_ids = jnp.arange(key_blocks, dtype=jnp.int32)
    owners, local_index = locate(lists, half_rows, group_width)
    distance = (my_index - owners) % group_width
    remote_mask = owners != my_index
    reach_ids = jnp.arange(1, DEVICES_BEHIND + 1, dtype=jnp.int32)
    match_reach = (distance.reshape(-1)[:, None] == reach_ids[None, :]) & remote_mask.reshape(-1)[
        :, None
    ]
    match_block = local_index.reshape(-1)[:, None] == block_ids[None, :]
    wanted = jnp.any(match_reach[:, :, None] & match_block[:, None, :], axis=0)
    requested, slot_rank = pick_slots(wanted, MAX_REMOTE_KEYS)
    reach_row = jnp.maximum(distance - 1, 0)
    slot_index = reach_row * MAX_REMOTE_KEYS + slot_rank[reach_row, local_index]
    table_index = jnp.where(remote_mask, slot_index, remote_slots + local_index)
    local_keys = fields[1].reshape(key_blocks, KBLK, channels)
    local_values = fields[2].reshape(key_blocks, KBLK, channels)
    served_rows = []
    fetched_keys = []
    fetched_values = []
    for reach_step in range(1, DEVICES_BEHIND + 1):
        served = passed_along(requested[reach_step - 1], "ctx", -reach_step)
        pick_rows = jnp.maximum(served, 0)
        got_keys, got_values = passed_along(
            (local_keys[pick_rows], local_values[pick_rows]), "ctx", reach_step
        )
        served_rows.append(served)
        fetched_keys.append(got_keys)
        fetched_values.append(got_values)
    served_all = jnp.stack(served_rows)
    head_count = channels // HEAD
    key_table = jnp.concatenate(
        [jnp.stack(fetched_keys).reshape(remote_slots * KBLK, channels), fields[1]], axis=0
    ).reshape(-1, head_count, HEAD)
    value_table = jnp.concatenate(
        [jnp.stack(fetched_values).reshape(remote_slots * KBLK, channels), fields[2]], axis=0
    ).reshape(-1, head_count, HEAD)
    scale_factor = HEAD ** (-0.5)
    slot_match = table_index[:, :, None] == jnp.arange(slots_total, dtype=jnp.int32)[None, None, :]
    member = jnp.any(slot_match, axis=1)
    slot_block = jnp.max(jnp.where(slot_match, lists[:, :, None], -1), axis=(0, 1))
    key_pos = (slot_block[:, None] * KBLK + jnp.arange(KBLK, dtype=jnp.int32)[None, :]).reshape(-1)
    named = jnp.repeat(jnp.repeat(member, QBLK, axis=0), KBLK, axis=1)
    visible = named & (key_pos[None, :] <= positions[:, None])
    query_heads = fields[0].reshape(tok_rows, head_count, HEAD)
    grad_heads = out_grad[0].reshape(tok_rows, head_count, HEAD)
    group_heads = math.gcd(head_count, 8)
    group_count = head_count // group_heads

    def as_slots(pieces):
        return jnp.concatenate(pieces, axis=1).reshape(slots_total, KBLK * channels)

    value_pieces = []
    query_pieces = []
    key_pieces = []
    for group_no in range(group_count):
        probabilities_first = group_no * group_heads
        probabilities_last = probabilities_first + group_heads
        scores = (
            jnp.einsum(
                "qhd,khd->hqk",
                query_heads[:, probabilities_first:probabilities_last],
                key_table[:, probabilities_first:probabilities_last],
                preferred_element_type=jnp.float32,
            )
            * scale_factor
        )
        scores = jnp.where(visible[None], scores, -jnp.inf)
        row_max = jnp.max(scores, axis=-1, keepdims=True)
        log_total = row_max + jnp.log(jnp.sum(jnp.exp(scores - row_max), axis=-1, keepdims=True))
        attn_probs = jnp.where(visible[None], jnp.exp(scores - log_total), 0.0)
        value_first = group_no * group_heads
        value_last = value_first + group_heads
        value_probs_half = attn_probs.astype(jnp.bfloat16)
        value_pieces.append(
            jnp.einsum(
                "hqk,qhd->khd",
                value_probs_half,
                grad_heads[:, value_first:value_last],
                preferred_element_type=jnp.float32,
            )
        )
        first = group_no * group_heads
        last = first + group_heads
        probs_half = attn_probs.astype(jnp.bfloat16)
        value_rows = value_table[:, first:last]
        key_rows = key_table[:, first:last]
        grads_here = grad_heads[:, first:last]
        outputs = jnp.einsum(
            "hqk,khd->qhd", probs_half, value_rows, preferred_element_type=jnp.float32
        )
        delta_rows = jnp.sum(outputs * grads_here.astype(jnp.float32), axis=-1)
        prob_grads = jnp.einsum(
            "qhd,khd->hqk", grads_here, value_rows, preferred_element_type=jnp.float32
        )
        score_grads = (
            attn_probs * (prob_grads - jnp.transpose(delta_rows, (1, 0))[..., None])
        ).astype(jnp.bfloat16)
        query_grads = (
            jnp.einsum("hqk,khd->qhd", score_grads, key_rows, preferred_element_type=jnp.float32)
            * scale_factor
        )
        key_terms = (
            jnp.einsum(
                "hqk,qhd->khd",
                score_grads,
                query_heads[:, first:last],
                preferred_element_type=jnp.float32,
            )
            * scale_factor
        )
        query_grads, key_terms = (query_grads, key_terms)
        query_pieces.append(query_grads)
        key_pieces.append(key_terms)
    value_slots = as_slots(value_pieces)
    key_slots = as_slots(key_pieces)
    query_all = jnp.concatenate(query_pieces, axis=1)
    key_out = key_slots[:remote_slots].reshape(DEVICES_BEHIND, MAX_REMOTE_KEYS, -1)
    value_out = value_slots[:remote_slots].reshape(DEVICES_BEHIND, MAX_REMOTE_KEYS, -1)
    key_parts = []
    value_parts = []
    for reach_step in range(1, DEVICES_BEHIND + 1):
        key_piece, value_piece = (
            passed_along(key_out[reach_step - 1].astype(jnp.bfloat16), "ctx", -reach_step).astype(
                jnp.float32
            ),
            passed_along(value_out[reach_step - 1].astype(jnp.bfloat16), "ctx", -reach_step).astype(
                jnp.float32
            ),
        )
        key_parts.append(key_piece)
        value_parts.append(value_piece)
    key_back = jnp.stack(key_parts)
    value_back = jnp.stack(value_parts)
    targets = jnp.where(served_all >= 0, served_all, key_blocks).reshape(-1)
    key_recv = jax.ops.segment_sum(
        key_back.reshape(remote_slots, -1), targets, num_segments=key_blocks + 1
    )[:key_blocks]
    value_recv = jax.ops.segment_sum(
        value_back.reshape(remote_slots, -1), targets, num_segments=key_blocks + 1
    )[:key_blocks]
    key_grads = (key_slots[remote_slots:] + key_recv).reshape(tok_rows, channels)
    value_grads = (value_slots[remote_slots:] + value_recv).reshape(tok_rows, channels)
    grad_rows = jnp.stack([query_all.reshape(tok_rows, channels), key_grads, value_grads])
    grad_edge = jnp.concatenate(
        [grad_rows[:, :rim_rows], grad_rows[:, half_rows : half_rows + rim_rows]], axis=1
    )
    grad_edged = with_halo(for_sending(grad_edge), (("ctx", 1),), rim_rows).astype(grad_edge.dtype)
    after_high = grad_edged[:, :rim_rows]
    after_low = jnp.where(
        is_last, grad_rows[:, half_rows : half_rows + rim_rows], grad_edged[:, 3 * rim_rows :]
    )
    grad_low = jnp.concatenate([grad_rows[:, :half_rows], after_low], axis=1)
    grad_high = jnp.concatenate([grad_rows[:, half_rows:], after_high], axis=1)
    input_grads = jnp.concatenate(
        [
            unconvolve(grad_low, conv_weight, half_rows),
            unconvolve(grad_high, conv_weight, half_rows),
        ],
        axis=1,
    ).astype(jnp.bfloat16)
    kernel_terms = tap_sums(grad_rows[:, :half_rows], extended_low) + tap_sums(
        grad_rows[:, half_rows:], extended_high
    )
    kernel_grad = lax.psum(kernel_terms, ("dp", "ctx"))
    return (input_grads[0][None], input_grads[1][None], input_grads[2][None], kernel_grad)


def solution(mesh):
    placed = (
        P("dp", "ctx", None),
        P("dp", "ctx", None),
        P("dp", "ctx", None),
        P(),
        P("dp", "ctx", None),
        P("dp", "ctx", None),
    )
    return jax.shard_map(
        body,
        mesh=mesh,
        in_specs=placed,
        out_specs=(P("dp", "ctx", None), P("dp", "ctx", None), P("dp", "ctx", None), P()),
        check_vma=False,
    )
```

profile of v0, /device:TPU:8, one launch (start us, length us, event | category | flops | bytes accessed | tf_op | source)
XLA Modules:
  0.0 1157.5 jit_solution(11848221441150544124)
XLA Ops:
  99.6 21.9 %collective-permute-done.7 = bf16[2,64,2048]{2,1,0:T(8,128)(2,1)} collective-permute-done((bf16[2,64,2048]{2,1,0:T(8,128)(2,1)}, bf16[2,64,2048]{2,1,0:T(8,128)(2,1)}, u32[]{:S(2)}, u32[]{:S(2)}) %collective-permute-start.7) | collective-permute-done | bytes 524320 | tf_op jit(solution)/shard_map/ppermute | solution.py:31
  167.6 33.2 %collective-permute-done.16 = bf16[2,64,2048]{2,1,0:T(8,128)(2,1)} collective-permute-done((bf16[2,64,2048]{2,1,0:T(8,128)(2,1)}, bf16[2,64,2048]{2,1,0:T(8,128)(2,1)}, u32[]{:S(2)}, u32[]{:S(2)}) %collective-permute-start.16) | collective-permute-done | bytes 524320 | tf_op jit(solution)/shard_map/ppermute | solution.py:31
  261.9 26.9 %collective-permute-start.27 = (bf16[2,131072]{1,0:T(2,128)(2,1)}, bf16[2,131072]{1,0:T(2,128)(2,1)}, u32[]{:S(2)}, u32[]{:S(2)}) collective-permute-start(bf16[2,131072]{1,0:T(2,128)(2,1)} %convert_element_type.111), channel_id=1, source_target_pairs={{0,62},{1,63},{2,0},{3,1},{4,2},{5,3},{6,4},{7,5},{8,6},{9,7},{10,... | collective-permute-start | bytes 1572872 | tf_op jit(solution)/shard_map/ppermute | solution.py:31
  371.8 228.1 %while.3 = (s32[]{:T(128)}, f32[5,131072]{1,0:T(8,128)}, s32[12]{0:T(128)S(1)}, f32[12,131072]{1,0:T(8,128)}, s32[]{:T(128)}, /*index=5*/s32[2]{0:T(128)S(1)}, s32[1]{0:T(128)}, s32[]{:T(128)}) while((s32[]{:T(128)}, f32[5,131072]{1,0:T(8,128)}, s32[12]{0:T(128)S(1)}, f32[12,131072]{1,0:T(8,128)}, s32[]{:T(128)}, /*index=5*/s32[2]{0:T(128)S(1)}, ...), condition=%wide.while_cond.1, body=%wide.while_body.1.sunk | while | flops 262155 | bytes 2621575 | solution.py:263
  379.3 11.5 dynamic-update-slice.61
  398.3 11.5 dynamic-update-slice.61
  417.3 11.5 dynamic-update-slice.61
  436.3 11.5 dynamic-update-slice.61
  455.3 11.5 dynamic-update-slice.61
  474.4 11.5 dynamic-update-slice.61
  493.4 11.5 dynamic-update-slice.61
  512.4 11.5 dynamic-update-slice.61
  531.4 11.5 dynamic-update-slice.61
  550.4 11.5 dynamic-update-slice.61
  569.4 11.5 dynamic-update-slice.61
  588.4 11.5 dynamic-update-slice.61
  604.7 19.7 %collective-permute-start.25 = (bf16[2,131072]{1,0:T(2,128)(2,1)S(1)}, bf16[2,131072]{1,0:T(2,128)(2,1)}, u32[]{:S(2)}, u32[]{:S(2)}) collective-permute-start(bf16[2,131072]{1,0:T(2,128)(2,1)S(1)} %copy-done.23), channel_id=1, source_target_pairs={{0,58},{1,59},{2,60},{3,61},{4,62},{5,63},{6,0},{7,1},{8,2},{9,3},... | collective-permute-start | bytes 1572872 | tf_op jit(solution)/shard_map/ppermute | solution.py:31
  642.1 8.9 reshape.530
  653.3 228.1 %while.2 = (s32[]{:T(128)}, f32[5,131072]{1,0:T(8,128)}, s32[12]{0:T(128)S(1)}, f32[12,131072]{1,0:T(8,128)}, s32[]{:T(128)}, /*index=5*/s32[2]{0:T(128)S(1)}, s32[1]{0:T(128)}, s32[]{:T(128)}) while((s32[]{:T(128)}, f32[5,131072]{1,0:T(8,128)}, s32[12]{0:T(128)S(1)}, f32[12,131072]{1,0:T(8,128)}, s32[]{:T(128)}, /*index=5*/s32[2]{0:T(128)S(1)}, ...), condition=%wide.while_cond, body=%wide.while_body.sunk | while | flops 262155 | bytes 2621575 | solution.py:260
  660.8 11.5 dynamic-update-slice.60
  679.8 11.5 dynamic-update-slice.60
  698.8 11.5 dynamic-update-slice.60
  717.8 11.5 dynamic-update-slice.60
  736.8 11.5 dynamic-update-slice.60
  755.8 11.5 dynamic-update-slice.60
  774.9 11.5 dynamic-update-slice.60
  793.9 11.5 dynamic-update-slice.60
  812.9 11.5 dynamic-update-slice.60
  831.9 11.5 dynamic-update-slice.60
  850.9 11.5 dynamic-update-slice.60
  869.9 11.5 dynamic-update-slice.60
  918.0 230.6 %all-reduce.2.cloned.1.call-done = f32[3,4,2048]{2,0,1:T(4,128)} async-done(((f32[3,4,2048]{2,0,1:T(4,128)}), f32[3,4,2048]{2,0,1:T(4,128)}) %all-reduce.2.cloned.1.call-update) | async-done | bytes 98320 | tf_op jit(solution)/shard_map/psum | solution.py:289
  (408 shorter events, 524.9 us)
Async XLA Ops:
  7.2 1141.4 %all-reduce.2.cloned.1.call-start = ((), (), s32[]{:S(2)}) async-start(), calls=%async_computation | async-start | bytes 262144 | tf_op jit(solution)/shard_map/psum | solution.py:289
  12.3 41.6 %collective-permute-start.1 = (bf16[3,3,2048]{2,1,0:T(4,128)(2,1)}, bf16[3,3,2048]{2,1,0:T(4,128)(2,1)}, u32[]{:S(2)}, u32[]{:S(2)}) collective-permute-start(bf16[3,3,2048]{2,1,0:T(4,128)(2,1)} %slice.390), channel_id=1, source_target_pairs={{1,0},{2,1},{3,2},{4,3},{5,4},{6,5},{7,6},{8,7},{9,8},{10,9},{11,1... | collective-permute-start | bytes 110600 | tf_op jit(solution)/shard_map/ppermute | solution.py:24
  15.9 28.2 %collective-permute-start.4 = (s32[2]{0:T(128)}, s32[2]{0:T(128)S(1)}, u32[]{:S(2)}, u32[]{:S(2)}) collective-permute-start(s32[2]{0:T(128)} %get-tuple-element.60), channel_id=1, source_target_pairs={{0,62},{1,63},{2,0},{3,1},{4,2},{5,3},{6,4},{7,5},{8,6},{9,7},{10,... | collective-permute-start | bytes 32 | tf_op jit(solution)/shard_map/ppermute | solution.py:31
  17.5 26.8 %collective-permute-start.2 = (s32[2]{0:T(128)}, s32[2]{0:T(128)}, u32[]{:S(2)}, u32[]{:S(2)}) collective-permute-start(s32[2]{0:T(128)} %get-tuple-element.61), channel_id=1, source_target_pairs={{0,63},{1,0},{2,1},{3,2},{4,3},{5,4},{6,5},{7,6},{8,7},{9,8},{10,9... | collective-permute-start | bytes 32 | tf_op jit(solution)/shard_map/ppermute | solution.py:31
  25.1 20.3 %collective-permute-start.8 = (s32[2]{0:T(128)}, s32[2]{0:T(128)S(1)}, u32[]{:S(2)}, u32[]{:S(2)}) collective-permute-start(s32[2]{0:T(128)} %get-tuple-element.58), channel_id=1, source_target_pairs={{0,60},{1,61},{2,62},{3,63},{4,0},{5,1},{6,2},{7,3},{8,4},{9,5},{1... | collective-permute-start | bytes 32 | tf_op jit(solution)/shard_map/ppermute | solution.py:31
  25.1 20.3 %collective-permute-start.6 = (s32[2]{0:T(128)}, s32[2]{0:T(128)S(1)}, u32[]{:S(2)}, u32[]{:S(2)}) collective-permute-start(s32[2]{0:T(128)} %get-tuple-element.59), channel_id=1, source_target_pairs={{0,61},{1,62},{2,63},{3,0},{4,1},{5,2},{6,3},{7,4},{8,5},{9,6},{10... | collective-permute-start | bytes 32 | tf_op jit(solution)/shard_map/ppermute | solution.py:31
  66.4 30.9 %collective-permute-start.3 = (bf16[2,64,2048]{2,1,0:T(8,128)(2,1)}, bf16[2,64,2048]{2,1,0:T(8,128)(2,1)}, u32[]{:S(2)}, u32[]{:S(2)}) collective-permute-start(bf16[2,64,2048]{2,1,0:T(8,128)(2,1)} %gather_fusion), channel_id=1, source_target_pairs={{0,1},{1,2},{2,3},{3,4},{4,5},{5,6},{6,7},{7,8},{8,9},{9,10},{10,1... | collective-permute-start | bytes 1572872 | tf_op jit(solution)/shard_map/ppermute | solution.py:31
  67.9 30.5 %collective-permute-start.5 = (bf16[2,64,2048]{2,1,0:T(8,128)(2,1)}, bf16[2,64,2048]{2,1,0:T(8,128)(2,1)}, u32[]{:S(2)}, u32[]{:S(2)}) collective-permute-start(bf16[2,64,2048]{2,1,0:T(8,128)(2,1)} %gather_fusion.1), channel_id=1, source_target_pairs={{0,2},{1,3},{2,4},{3,5},{4,6},{5,7},{6,8},{7,9},{8,10},{9,11},{10,... | collective-permute-start | bytes 1572872 | tf_op jit(solution)/shard_map/ppermute | solution.py:31
  87.5 33.9 %collective-permute-start.7 = (bf16[2,64,2048]{2,1,0:T(8,128)(2,1)}, bf16[2,64,2048]{2,1,0:T(8,128)(2,1)}, u32[]{:S(2)}, u32[]{:S(2)}) collective-permute-start(bf16[2,64,2048]{2,1,0:T(8,128)(2,1)} %gather_fusion.2), channel_id=1, source_target_pairs={{0,3},{1,4},{2,5},{3,6},{4,7},{5,8},{6,9},{7,10},{8,11},{9,12},{10... | collective-permute-start | bytes 1572872 | tf_op jit(solution)/shard_map/ppermute | solution.py:31
  92.6 31.2 %collective-permute-start.9 = (bf16[2,64,2048]{2,1,0:T(8,128)(2,1)}, bf16[2,64,2048]{2,1,0:T(8,128)(2,1)}, u32[]{:S(2)}, u32[]{:S(2)}) collective-permute-start(bf16[2,64,2048]{2,1,0:T(8,128)(2,1)} %gather_fusion.3), channel_id=1, source_target_pairs={{0,4},{1,5},{2,6},{3,7},{4,8},{5,9},{6,10},{7,11},{8,12},{9,13},{1... | collective-permute-start | bytes 1572872 | tf_op jit(solution)/shard_map/ppermute | solution.py:31
  92.6 40.2 %collective-permute-start.11 = (bf16[2,64,2048]{2,1,0:T(8,128)(2,1)}, bf16[2,64,2048]{2,1,0:T(8,128)(2,1)S(1)}, u32[]{:S(2)}, u32[]{:S(2)}) collective-permute-start(bf16[2,64,2048]{2,1,0:T(8,128)(2,1)} %gather_fusion.4), channel_id=1, source_target_pairs={{0,5},{1,6},{2,7},{3,8},{4,9},{5,10},{6,11},{7,12},{8,13},{9,14},{... | collective-permute-start | bytes 1572872 | tf_op jit(solution)/shard_map/ppermute | solution.py:31
  97.3 40.5 %collective-permute-start.13 = (bf16[2,64,2048]{2,1,0:T(8,128)(2,1)}, bf16[2,64,2048]{2,1,0:T(8,128)(2,1)S(1)}, u32[]{:S(2)}, u32[]{:S(2)}) collective-permute-start(bf16[2,64,2048]{2,1,0:T(8,128)(2,1)} %gather_fusion.5), channel_id=1, source_target_pairs={{0,6},{1,7},{2,8},{3,9},{4,10},{5,11},{6,12},{7,13},{8,14},{9,15},... | collective-permute-start | bytes 1572872 | tf_op jit(solution)/shard_map/ppermute | solution.py:31
  98.4 59.3 %collective-permute-start.14 = (bf16[2,64,2048]{2,1,0:T(8,128)(2,1)}, bf16[2,64,2048]{2,1,0:T(8,128)(2,1)S(1)}, u32[]{:S(2)}, u32[]{:S(2)}) collective-permute-start(bf16[2,64,2048]{2,1,0:T(8,128)(2,1)} %gather_fusion.7), channel_id=1, source_target_pairs={{0,1},{1,2},{2,3},{3,4},{4,5},{5,6},{6,7},{7,8},{8,9},{9,10},{10,1... | collective-permute-start | bytes 1572872 | tf_op jit(solution)/shard_map/ppermute | solution.py:31
  121.5 43.7 %collective-permute-start.15 = (bf16[2,64,2048]{2,1,0:T(8,128)(2,1)}, bf16[2,64,2048]{2,1,0:T(8,128)(2,1)}, u32[]{:S(2)}, u32[]{:S(2)}) collective-permute-start(bf16[2,64,2048]{2,1,0:T(8,128)(2,1)} %gather_fusion.8), channel_id=1, source_target_pairs={{0,2},{1,3},{2,4},{3,5},{4,6},{5,7},{6,8},{7,9},{8,10},{9,11},{10,... | collective-permute-start | bytes 1572872 | tf_op jit(solution)/shard_map/ppermute | solution.py:31
  123.8 77.0 %collective-permute-start.16 = (bf16[2,64,2048]{2,1,0:T(8,128)(2,1)}, bf16[2,64,2048]{2,1,0:T(8,128)(2,1)}, u32[]{:S(2)}, u32[]{:S(2)}) collective-permute-start(bf16[2,64,2048]{2,1,0:T(8,128)(2,1)} %gather_fusion.9), channel_id=1, source_target_pairs={{0,3},{1,4},{2,5},{3,6},{4,7},{5,8},{6,9},{7,10},{8,11},{9,12},{10... | collective-permute-start | bytes 1572872 | tf_op jit(solution)/shard_map/ppermute | solution.py:31
  132.8 70.0 %collective-permute-start.17 = (bf16[2,64,2048]{2,1,0:T(8,128)(2,1)}, bf16[2,64,2048]{2,1,0:T(8,128)(2,1)}, u32[]{:S(2)}, u32[]{:S(2)}) collective-permute-start(bf16[2,64,2048]{2,1,0:T(8,128)(2,1)} %gather_fusion.10), channel_id=1, source_target_pairs={{0,4},{1,5},{2,6},{3,7},{4,8},{5,9},{6,10},{7,11},{8,12},{9,13},{1... | collective-permute-start | bytes 1572872 | tf_op jit(solution)/shard_map/ppermute | solution.py:31
  137.8 68.3 %collective-permute-start.18 = (bf16[2,64,2048]{2,1,0:T(8,128)(2,1)}, bf16[2,64,2048]{2,1,0:T(8,128)(2,1)}, u32[]{:S(2)}, u32[]{:S(2)}) collective-permute-start(bf16[2,64,2048]{2,1,0:T(8,128)(2,1)} %gather_fusion.11), channel_id=1, source_target_pairs={{0,5},{1,6},{2,7},{3,8},{4,9},{5,10},{6,11},{7,12},{8,13},{9,14},{... | collective-permute-start | bytes 1572872 | tf_op jit(solution)/shard_map/ppermute | solution.py:31
  157.8 50.8 %collective-permute-start.19 = (bf16[2,64,2048]{2,1,0:T(8,128)(2,1)}, bf16[2,64,2048]{2,1,0:T(8,128)(2,1)}, u32[]{:S(2)}, u32[]{:S(2)}) collective-permute-start(bf16[2,64,2048]{2,1,0:T(8,128)(2,1)} %gather_fusion.12), channel_id=1, source_target_pairs={{0,6},{1,7},{2,8},{3,9},{4,10},{5,11},{6,12},{7,13},{8,14},{9,15},... | collective-permute-start | bytes 1572872 | tf_op jit(solution)/shard_map/ppermute | solution.py:31
  242.8 97.1 %collective-permute-start.26 = (bf16[2,131072]{1,0:T(2,128)(2,1)}, bf16[2,131072]{1,0:T(2,128)(2,1)}, u32[]{:S(2)}, u32[]{:S(2)}) collective-permute-start(bf16[2,131072]{1,0:T(2,128)(2,1)} %convert_element_type.110), channel_id=1, source_target_pairs={{0,63},{1,0},{2,1},{3,2},{4,3},{5,4},{6,5},{7,6},{8,7},{9,8},{10,9... | collective-permute-start | bytes 1572872 | tf_op jit(solution)/shard_map/ppermute | solution.py:31
  261.9 82.8 %collective-permute-start.27 = (bf16[2,131072]{1,0:T(2,128)(2,1)}, bf16[2,131072]{1,0:T(2,128)(2,1)}, u32[]{:S(2)}, u32[]{:S(2)}) collective-permute-start(bf16[2,131072]{1,0:T(2,128)(2,1)} %convert_element_type.111), channel_id=1, source_target_pairs={{0,62},{1,63},{2,0},{3,1},{4,2},{5,3},{6,4},{7,5},{8,6},{9,7},{10,... | collective-permute-start | bytes 1572872 | tf_op jit(solution)/shard_map/ppermute | solution.py:31
  292.9 54.6 %collective-permute-start.28 = (bf16[2,131072]{1,0:T(2,128)(2,1)}, bf16[2,131072]{1,0:T(2,128)(2,1)}, u32[]{:S(2)}, u32[]{:S(2)}) collective-permute-start(bf16[2,131072]{1,0:T(2,128)(2,1)} %convert_element_type.112), channel_id=1, source_target_pairs={{0,61},{1,62},{2,63},{3,0},{4,1},{5,2},{6,3},{7,4},{8,5},{9,6},{10... | collective-permute-start | bytes 1572872 | tf_op jit(solution)/shard_map/ppermute | solution.py:31
  297.5 54.3 %collective-permute-start.29 = (bf16[2,131072]{1,0:T(2,128)(2,1)}, bf16[2,131072]{1,0:T(2,128)(2,1)}, u32[]{:S(2)}, u32[]{:S(2)}) collective-permute-start(bf16[2,131072]{1,0:T(2,128)(2,1)} %convert_element_type.113), channel_id=1, source_target_pairs={{0,60},{1,61},{2,62},{3,63},{4,0},{5,1},{6,2},{7,3},{8,4},{9,5},{1... | collective-permute-start | bytes 1572872 | tf_op jit(solution)/shard_map/ppermute | solution.py:31
  300.6 53.4 %collective-permute-start.30 = (bf16[2,131072]{1,0:T(2,128)(2,1)}, bf16[2,131072]{1,0:T(2,128)(2,1)}, u32[]{:S(2)}, u32[]{:S(2)}) collective-permute-start(bf16[2,131072]{1,0:T(2,128)(2,1)} %convert_element_type.114), channel_id=1, source_target_pairs={{0,59},{1,60},{2,61},{3,62},{4,63},{5,0},{6,1},{7,2},{8,3},{9,4},{... | collective-permute-start | bytes 1572872 | tf_op jit(solution)/shard_map/ppermute | solution.py:31
  340.0 18.9 %collective-permute-start.31 = (bf16[2,131072]{1,0:T(2,128)(2,1)S(1)}, bf16[2,131072]{1,0:T(2,128)(2,1)S(1)}, u32[]{:S(2)}, u32[]{:S(2)}) collective-permute-start(bf16[2,131072]{1,0:T(2,128)(2,1)S(1)} %copy-done.25), channel_id=1, source_target_pairs={{0,58},{1,59},{2,60},{3,61},{4,62},{5,63},{6,0},{7,1},{8,2},{9,3},... | collective-permute-start | bytes 1572872 | tf_op jit(solution)/shard_map/ppermute | solution.py:31
  344.7 259.9 %collective-permute-start.20 = (bf16[2,131072]{1,0:T(2,128)(2,1)}, bf16[2,131072]{1,0:T(2,128)(2,1)}, u32[]{:S(2)}, u32[]{:S(2)}) collective-permute-start(bf16[2,131072]{1,0:T(2,128)(2,1)} %convert_element_type.104), channel_id=1, source_target_pairs={{0,63},{1,0},{2,1},{3,2},{4,3},{5,4},{6,5},{7,6},{8,7},{9,8},{10,9... | collective-permute-start | bytes 1572872 | tf_op jit(solution)/shard_map/ppermute | solution.py:31
  347.5 279.2 %collective-permute-start.21 = (bf16[2,131072]{1,0:T(2,128)(2,1)}, bf16[2,131072]{1,0:T(2,128)(2,1)}, u32[]{:S(2)}, u32[]{:S(2)}) collective-permute-start(bf16[2,131072]{1,0:T(2,128)(2,1)} %convert_element_type.105), channel_id=1, source_target_pairs={{0,62},{1,63},{2,0},{3,1},{4,2},{5,3},{6,4},{7,5},{8,6},{9,7},{10,... | collective-permute-start | bytes 1572872 | tf_op jit(solution)/shard_map/ppermute | solution.py:31
  351.8 277.1 %collective-permute-start.22 = (bf16[2,131072]{1,0:T(2,128)(2,1)}, bf16[2,131072]{1,0:T(2,128)(2,1)}, u32[]{:S(2)}, u32[]{:S(2)}) collective-permute-start(bf16[2,131072]{1,0:T(2,128)(2,1)} %convert_element_type.106), channel_id=1, source_target_pairs={{0,61},{1,62},{2,63},{3,0},{4,1},{5,2},{6,3},{7,4},{8,5},{9,6},{10... | collective-permute-start | bytes 1572872 | tf_op jit(solution)/shard_map/ppermute | solution.py:31
  354.0 277.0 %collective-permute-start.23 = (bf16[2,131072]{1,0:T(2,128)(2,1)}, bf16[2,131072]{1,0:T(2,128)(2,1)}, u32[]{:S(2)}, u32[]{:S(2)}) collective-permute-start(bf16[2,131072]{1,0:T(2,128)(2,1)} %convert_element_type.107), channel_id=1, source_target_pairs={{0,60},{1,61},{2,62},{3,63},{4,0},{5,1},{6,2},{7,3},{8,4},{9,5},{1... | collective-permute-start | bytes 1572872 | tf_op jit(solution)/shard_map/ppermute | solution.py:31
  358.8 274.5 %collective-permute-start.24 = (bf16[2,131072]{1,0:T(2,128)(2,1)S(1)}, bf16[2,131072]{1,0:T(2,128)(2,1)}, u32[]{:S(2)}, u32[]{:S(2)}) collective-permute-start(bf16[2,131072]{1,0:T(2,128)(2,1)S(1)} %copy-done.24), channel_id=1, source_target_pairs={{0,59},{1,60},{2,61},{3,62},{4,63},{5,0},{6,1},{7,2},{8,3},{9,4},{... | collective-permute-start | bytes 1572872 | tf_op jit(solution)/shard_map/ppermute | solution.py:31
  604.7 35.3 %collective-permute-start.25 = (bf16[2,131072]{1,0:T(2,128)(2,1)S(1)}, bf16[2,131072]{1,0:T(2,128)(2,1)}, u32[]{:S(2)}, u32[]{:S(2)}) collective-permute-start(bf16[2,131072]{1,0:T(2,128)(2,1)S(1)} %copy-done.23), channel_id=1, source_target_pairs={{0,58},{1,59},{2,60},{3,61},{4,62},{5,63},{6,0},{7,1},{8,2},{9,3},... | collective-permute-start | bytes 1572872 | tf_op jit(solution)/shard_map/ppermute | solution.py:31
  899.5 6.0 collective-permute-start.33
  901.4 5.5 collective-permute-start.32
  (49 other events, 291.1 us)
Sparse Core Ops, SparseCore 0:
  905.6 242.9 all-reduce.1
where the time goes:
time: 1180 us; the launch traced here: 1160 us
  local copies, waits for them, and re-layouts  478 us (41%)
  waiting for transfers between devices  304 us (26%)
  other arithmetic  223 us (19%)
  starting transfers between devices  100 us (8%)
  matrix products  36.7 us (3%)
  between operations  15.4 us (1%)
    scatter-add x48, local copies, waits for them, and re-layouts  290 us
    psum x1, waiting for transfers between devices, body(): kernel_grad = lax.psum(kernel_terms, ('dp', 'ctx'))  231 us
    scatter-add x48, other arithmetic  166 us
    ppermute x30, starting transfers between devices, passed_along(): return lax.ppermute(x, axis, [(i, (i + by) % count) for i in range(count)])  91.8 us
    ppermute x30, waiting for transfers between devices, passed_along(): return lax.ppermute(x, axis, [(i, (i + by) % count) for i in range(count)])  69.2 us
    unnamed x123, local copies, waits for them, and re-layouts  60.6 us
  transfers between devices with their start and end apart: 35, of which 9 were waited for; matrix products, arithmetic and copies ran while one was open for 37% of the time, Pallas kernels for 0%

commit v1 on v0

--- a/solution.py
+++ b/solution.py
@@ -29,6 +29,15 @@
 def passed_along(x, axis, by):
     count = lax.axis_size(axis)
     return lax.ppermute(x, axis, [(i, (i + by) % count) for i in range(count)])
+
+
+def summed_over(x, axis):
+    count = lax.axis_size(axis)
+    step = 1
+    while step < count:
+        x = x + lax.ppermute(x, axis, [(i, i ^ step) for i in range(count)])
+        step *= 2
+    return x
 
 
 def for_sending(x):
@@ -257,12 +266,19 @@
     key_back = jnp.stack(key_parts)
     value_back = jnp.stack(value_parts)
     targets = jnp.where(served_all >= 0, served_all, key_blocks).reshape(-1)
-    key_recv = jax.ops.segment_sum(
-        key_back.reshape(remote_slots, -1), targets, num_segments=key_blocks + 1
-    )[:key_blocks]
-    value_recv = jax.ops.segment_sum(
-        value_back.reshape(remote_slots, -1), targets, num_segments=key_blocks + 1
-    )[:key_blocks]
+
+    def placed_terms(back):
+        rows = back.reshape(remote_slots, -1)
+        sums = []
+        for block in range(key_blocks):
+            total = jnp.where(targets[0] == block, rows[0], 0.0)
+            for slot in range(1, remote_slots):
+                total = total + jnp.where(targets[slot] == block, rows[slot], 0.0)
+            sums.append(total)
+        return jnp.stack(sums)
+
+    key_recv = placed_terms(key_back)
+    value_recv = placed_terms(value_back)
     key_grads = (key_slots[remote_slots:] + key_recv).reshape(tok_rows, channels)
     value_grads = (value_slots[remote_slots:] + value_recv).reshape(tok_rows, channels)
     grad_rows = jnp.stack([query_all.reshape(tok_rows, channels), key_grads, value_grads])
@@ -286,7 +302,7 @@
     kernel_terms = tap_sums(grad_rows[:, :half_rows], extended_low) + tap_sums(
         grad_rows[:, half_rows:], extended_high
     )
-    kernel_grad = lax.psum(kernel_terms, ("dp", "ctx"))
+    kernel_grad = summed_over(summed_over(kernel_terms, "ctx"), "dp")
     return (input_grads[0][None], input_grads[1][None], input_grads[2][None], kernel_grad)
 
 

time: 1180 us -> 722 us (0.61)
  local copies, waits for them, and re-layouts: 478 us -> 152 us
  waiting for transfers between devices: 304 us -> 185 us
  other arithmetic: 223 us -> 160 us
  starting transfers between devices: 100 us -> 140 us
  between operations: 15.4 us -> 32.3 us
    scatter-add x48 -> x0, local copies, waits for them, and re-layouts: 290 us -> none
    psum x1 -> x0, waiting for transfers between devices: 231 us -> none  [body(): kernel_grad = lax.psum(kernel_terms, ('dp', 'ctx'))]
    scatter-add x48 -> x0, other arithmetic: 166 us -> none
    add x0 -> x16, other arithmetic: none -> 110 us  [the longest x8 108 us: placed_terms(): total = total + jnp.where(targets[slot] == block, rows[slot], 0.0)]
    ppermute x30, waiting for transfers between devices: 69.2 us -> 149 us  [passed_along(): return lax.ppermute(x, axis, [(i, (i + by) % count) for i in range(count)])]
    ppermute x0 -> x8, waiting for transfers between devices: none -> 31.6 us  [summed_over(): x = x + lax.ppermute(x, axis, [(i, i ^ step) for i in range(count)])]
    ppermute x30, starting transfers between devices: 91.8 us -> 120 us  [passed_along(): return lax.ppermute(x, axis, [(i, (i + by) % count) for i in range(count)])]
    unnamed x123 -> x127, local copies, waits for them, and re-layouts: 60.6 us -> 41.1 us
  transfers between devices with their start and end apart: 35 -> 42, of which waited for: 9 -> 20; matrix products, arithmetic and copies ran while one was open for 37% -> 19% of each run, Pallas kernels for 0% -> 0%
where the time goes in v1:
time: 722 us; the launch traced here: 710 us
  waiting for transfers between devices  185 us (26%)
  other arithmetic  160 us (22%)
  local copies, waits for them, and re-layouts  152 us (21%)
  starting transfers between devices  140 us (19%)
  matrix products  41.4 us (6%)
  between operations  32.3 us (4%)
    ppermute x30, waiting for transfers between devices, passed_along(): return lax.ppermute(x, axis, [(i, (i + by) % count) for i in range(count)])  149 us
    ppermute x30, starting transfers between devices, passed_along(): return lax.ppermute(x, axis, [(i, (i + by) % count) for i in range(count)])  120 us
    add x8, other arithmetic, placed_terms(): total = total + jnp.where(targets[slot] == block, rows[slot], 0.0)  108 us
    unnamed x127, local copies, waits for them, and re-layouts  41.1 us
    ppermute x8, waiting for transfers between devices, summed_over(): x = x + lax.ppermute(x, axis, [(i, i ^ step) for i in range(count)])  31.6 us
    reshape x2, local copies, waits for them, and re-layouts, placed_terms(): rows = back.reshape(remote_slots, -1)  17.4 us
  transfers between devices with their start and end apart: 42, of which 20 were waited for; matrix products, arithmetic and copies ran while one was open for 19% of the time, Pallas kernels for 0%

profile of v1, /device:TPU:8, one launch (start us, length us, event | category | flops | bytes accessed | tf_op | source)
XLA Modules:
  0.0 710.3 jit_solution(8747638140621306613)
XLA Ops:
  3.0 6.9 collective-permute-start.12
  115.3 12.5 %collective-permute-done.15 = bf16[2,64,2048]{2,1,0:T(8,128)(2,1)} collective-permute-done((bf16[2,64,2048]{2,1,0:T(8,128)(2,1)}, bf16[2,64,2048]{2,1,0:T(8,128)(2,1)}, u32[]{:S(2)}, u32[]{:S(2)}) %collective-permute-start.15) | collective-permute-done | bytes 524320 | tf_op jit(solution)/shard_map/ppermute | solution.py:31
  127.8 24.3 %collective-permute-start.17 = (bf16[2,64,2048]{2,1,0:T(8,128)(2,1)}, bf16[2,64,2048]{2,1,0:T(8,128)(2,1)S(1)}, u32[]{:S(2)}, u32[]{:S(2)}) collective-permute-start(bf16[2,64,2048]{2,1,0:T(8,128)(2,1)} %gather_fusion.10), channel_id=1, source_target_pairs={{0,4},{1,5},{2,6},{3,7},{4,8},{5,9},{6,10},{7,11},{8,12},{9,13},{1... | collective-permute-start | bytes 1572872 | tf_op jit(solution)/shard_map/ppermute | solution.py:31
  153.1 15.9 %collective-permute-done.16 = bf16[2,64,2048]{2,1,0:T(8,128)(2,1)S(1)} collective-permute-done((bf16[2,64,2048]{2,1,0:T(8,128)(2,1)}, bf16[2,64,2048]{2,1,0:T(8,128)(2,1)S(1)}, u32[]{:S(2)}, u32[]{:S(2)}) %collective-permute-start.16) | collective-permute-done | bytes 524320 | tf_op jit(solution)/shard_map/ppermute | solution.py:31
  174.1 24.9 %collective-permute-done.17 = bf16[2,64,2048]{2,1,0:T(8,128)(2,1)S(1)} collective-permute-done((bf16[2,64,2048]{2,1,0:T(8,128)(2,1)}, bf16[2,64,2048]{2,1,0:T(8,128)(2,1)S(1)}, u32[]{:S(2)}, u32[]{:S(2)}) %collective-permute-start.17) | collective-permute-done | bytes 524320 | tf_op jit(solution)/shard_map/ppermute | solution.py:31
  199.0 14.3 %collective-permute-start.11 = (bf16[2,64,2048]{2,1,0:T(8,128)(2,1)S(1)}, bf16[2,64,2048]{2,1,0:T(8,128)(2,1)S(1)}, u32[]{:S(2)}, u32[]{:S(2)}) collective-permute-start(bf16[2,64,2048]{2,1,0:T(8,128)(2,1)S(1)} %copy-done.28), channel_id=1, source_target_pairs={{0,5},{1,6},{2,7},{3,8},{4,9},{5,10},{6,11},{7,12},{8,13},{9,14},{... | collective-permute-start | bytes 1572872 | tf_op jit(solution)/shard_map/ppermute | solution.py:31
  213.3 6.6 collective-permute-done.19
  222.2 15.8 %collective-permute-done.11 = bf16[2,64,2048]{2,1,0:T(8,128)(2,1)S(1)} collective-permute-done((bf16[2,64,2048]{2,1,0:T(8,128)(2,1)S(1)}, bf16[2,64,2048]{2,1,0:T(8,128)(2,1)S(1)}, u32[]{:S(2)}, u32[]{:S(2)}) %collective-permute-start.11) | collective-permute-done | bytes 524320 | tf_op jit(solution)/shard_map/ppermute | solution.py:31
  262.4 6.2 fusion.2
  336.3 6.4 collective-permute-start.22
  373.8 23.4 %collective-permute-done.27 = bf16[2,131072]{1,0:T(2,128)(2,1)S(1)} collective-permute-done((bf16[2,131072]{1,0:T(2,128)(2,1)}, bf16[2,131072]{1,0:T(2,128)(2,1)S(1)}, u32[]{:S(2)}, u32[]{:S(2)}) %collective-permute-start.27) | collective-permute-done | bytes 524320 | tf_op jit(solution)/shard_map/ppermute | solution.py:31
  397.2 20.1 %collective-permute-start.28 = (bf16[2,131072]{1,0:T(2,128)(2,1)}, bf16[2,131072]{1,0:T(2,128)(2,1)S(1)}, u32[]{:S(2)}, u32[]{:S(2)}) collective-permute-start(bf16[2,131072]{1,0:T(2,128)(2,1)} %convert_element_type.112), channel_id=1, source_target_pairs={{0,61},{1,62},{2,63},{3,0},{4,1},{5,2},{6,3},{7,4},{8,5},{9,6},{10... | collective-permute-start | bytes 1572872 | tf_op jit(solution)/shard_map/ppermute | solution.py:31
  418.5 6.8 collective-permute-done.28
  425.3 10.7 %collective-permute-start.29 = (bf16[2,131072]{1,0:T(2,128)(2,1)S(1)}, bf16[2,131072]{1,0:T(2,128)(2,1)S(1)}, u32[]{:S(2)}, u32[]{:S(2)}) collective-permute-start(bf16[2,131072]{1,0:T(2,128)(2,1)S(1)} %copy-done.26), channel_id=1, source_target_pairs={{0,60},{1,61},{2,62},{3,63},{4,0},{5,1},{6,2},{7,3},{8,4},{9,5},{1... | collective-permute-start | bytes 1572872 | tf_op jit(solution)/shard_map/ppermute | solution.py:31
  437.1 15.0 %collective-permute-done.29 = bf16[2,131072]{1,0:T(2,128)(2,1)S(1)} collective-permute-done((bf16[2,131072]{1,0:T(2,128)(2,1)S(1)}, bf16[2,131072]{1,0:T(2,128)(2,1)S(1)}, u32[]{:S(2)}, u32[]{:S(2)}) %collective-permute-start.29) | collective-permute-done | bytes 524320 | tf_op jit(solution)/shard_map/ppermute | solution.py:31
  453.3 9.5 %collective-permute-done.30 = bf16[2,131072]{1,0:T(2,128)(2,1)S(1)} collective-permute-done((bf16[2,131072]{1,0:T(2,128)(2,1)S(1)}, bf16[2,131072]{1,0:T(2,128)(2,1)S(1)}, u32[]{:S(2)}, u32[]{:S(2)}) %collective-permute-start.30) | collective-permute-done | bytes 524320 | tf_op jit(solution)/shard_map/ppermute | solution.py:31
  464.3 8.2 %collective-permute-start.31 = (bf16[2,131072]{1,0:T(2,128)(2,1)S(1)}, bf16[2,131072]{1,0:T(2,128)(2,1)}, u32[]{:S(2)}, u32[]{:S(2)}) collective-permute-start(bf16[2,131072]{1,0:T(2,128)(2,1)S(1)} %copy-done.24), channel_id=1, source_target_pairs={{0,58},{1,59},{2,60},{3,61},{4,62},{5,63},{6,0},{7,1},{8,2},{9,3},... | collective-permute-start | bytes 1572872 | tf_op jit(solution)/shard_map/ppermute | solution.py:31
  480.3 14.7 %collective-permute-done.25 = bf16[2,131072]{1,0:T(2,128)(2,1)S(1)} collective-permute-done((bf16[2,131072]{1,0:T(2,128)(2,1)S(1)}, bf16[2,131072]{1,0:T(2,128)(2,1)S(1)}, u32[]{:S(2)}, u32[]{:S(2)}) %collective-permute-start.25) | collective-permute-done | bytes 524320 | tf_op jit(solution)/shard_map/ppermute | solution.py:31
  496.1 8.8 %reshape.611 = f32[12,131072]{1,0:T(8,128)} reshape(bf16[6,2,131072]{2,1,0:T(2,128)(2,1)} %bitcast_dynamic-update-slice_fusion.6) | data formatting | bytes 9437184 | tf_op jit(solution)/shard_map/reshape | solution.py:271
  507.2 8.6 %reshape.613 = f32[12,131072]{1,0:T(8,128)} reshape(bf16[6,2,131072]{2,1,0:T(2,128)(2,1)} %bitcast_dynamic-update-slice_fusion) | data formatting | bytes 9437184 | tf_op jit(solution)/shard_map/reshape | solution.py:271
  515.7 23.8 %fusion.89 = f32[1,131072]{1,0:T(1,128)S(1)} fusion(pred[]{:T(512)} %bitcast.55, pred[]{:T(512)} %bitcast.56, pred[]{:T(512)} %bitcast.54, pred[]{:T(512)} %bitcast.53, pred[]{:T(512)} %bitcast.52, pred[]{:T(512)} %bitcast.51, pred[]{:T(512)} %bitcast.50, pred[]{:T(512)} %bitcast.49, pred[]{:T(512)} %bitcast.48, pred[]{:T(512)} %bitcast.47, pred[]{:T(512)} %bitcast.46, ...), kind=kLoop, calls=%fused_computation.247 | loop fusion | flops 3014656 | bytes 6815756 | tf_op jit(solution)/shard_map/add | solution.py:276
  539.5 24.8 %fusion.91 = f32[1,131072]{1,0:T(1,128)S(1)} fusion(pred[]{:T(512)} %bitcast.55, pred[]{:T(512)} %bitcast.56, pred[]{:T(512)} %bitcast.54, pred[]{:T(512)} %bitcast.53, pred[]{:T(512)} %bitcast.52, pred[]{:T(512)} %bitcast.51, pred[]{:T(512)} %bitcast.50, pred[]{:T(512)} %bitcast.49, pred[]{:T(512)} %bitcast.48, pred[]{:T(512)} %bitcast.47, pred[]{:T(512)} %bitcast.46, ...), kind=kLoop, calls=%fused_computation.249 | loop fusion | flops 3014656 | bytes 6815756 | tf_op jit(solution)/shard_map/add | solution.py:276
  564.4 24.5 %fusion.111 = f32[1,131072]{1,0:T(1,128)} fusion(pred[]{:T(512)} %bitcast.67, pred[]{:T(512)} %bitcast.68, pred[]{:T(512)} %bitcast.66, pred[]{:T(512)} %bitcast.65, pred[]{:T(512)} %bitcast.64, pred[]{:T(512)} %bitcast.63, pred[]{:T(512)} %bitcast.62, pred[]{:T(512)} %bitcast.61, pred[]{:T(512)} %bitcast.60, pred[]{:T(512)} %bitcast.59, pred[]{:T(512)} %bitcast.58, ...), kind=kLoop, calls=%fused_computation.269 | loop fusion | flops 3014656 | bytes 6815756 | tf_op jit(solution)/shard_map/add | solution.py:276
  588.9 6.5 fusion.113
  595.4 7.1 %fusion.133 = f32[1,131072]{1,0:T(1,128)} fusion(pred[]{:T(512)} %bitcast.79, pred[]{:T(512)} %bitcast.80, pred[]{:T(512)} %bitcast.78, pred[]{:T(512)} %bitcast.77, pred[]{:T(512)} %bitcast.76, pred[]{:T(512)} %bitcast.75, pred[]{:T(512)} %bitcast.74, pred[]{:T(512)} %bitcast.73, pred[]{:T(512)} %bitcast.72, pred[]{:T(512)} %bitcast.71, pred[]{:T(512)} %bitcast.70, ...), kind=kLoop, calls=%fused_computation.291 | loop fusion | flops 3014656 | bytes 6815756 | tf_op jit(solution)/shard_map/add | solution.py:276
  602.6 7.1 fusion.135
  609.7 7.1 fusion.155
  616.8 7.3 %fusion.157 = f32[1,131072]{1,0:T(1,128)} fusion(pred[]{:T(512)} %bitcast.91, pred[]{:T(512)} %bitcast.92, pred[]{:T(512)} %bitcast.90, pred[]{:T(512)} %bitcast.89, pred[]{:T(512)} %bitcast.88, pred[]{:T(512)} %bitcast.87, pred[]{:T(512)} %bitcast.86, pred[]{:T(512)} %bitcast.85, pred[]{:T(512)} %bitcast.84, pred[]{:T(512)} %bitcast.83, pred[]{:T(512)} %bitcast.82, ...), kind=kLoop, calls=%fused_computation.315 | loop fusion | flops 3014656 | bytes 6815756 | tf_op jit(solution)/shard_map/add | solution.py:276
  656.8 5.5 collective-permute-done.35
  663.5 6.5 collective-permute-done.36
  679.7 7.0 collective-permute-done.38
  686.9 10.1 %collective-permute-done.39 = f32[3,4,2048]{2,0,1:T(4,128)S(1)} collective-permute-done((f32[3,4,2048]{2,0,1:T(4,128)S(1)}, f32[3,4,2048]{2,0,1:T(4,128)S(1)}, u32[]{:S(2)}, u32[]{:S(2)}) %collective-permute-start.39) | collective-permute-done | bytes 98336 | tf_op jit(solution)/shard_map/ppermute | solution.py:38
  (342 shorter events, 281.3 us)
Async XLA Ops:
  3.0 31.1 %collective-permute-start.12 = (s32[2]{0:T(128)}, s32[2]{0:T(128)S(1)}, u32[]{:S(2)}, u32[]{:S(2)}) collective-permute-start(s32[2]{0:T(128)} %get-tuple-element.40), channel_id=1, source_target_pairs={{0,58},{1,59},{2,60},{3,61},{4,62},{5,63},{6,0},{7,1},{8,2},{9,3},... | collective-permute-start | bytes 32 | tf_op jit(solution)/shard_map/ppermute | solution.py:31
  9.9 24.4 %collective-permute-start.10 = (s32[2]{0:T(128)S(1)}, s32[2]{0:T(128)S(1)}, u32[]{:S(2)}, u32[]{:S(2)}) collective-permute-start(s32[2]{0:T(128)S(1)} %get-tuple-element.41), channel_id=1, source_target_pairs={{0,59},{1,60},{2,61},{3,62},{4,63},{5,0},{6,1},{7,2},{8,3},{9,4},{... | collective-permute-start | bytes 32 | tf_op jit(solution)/shard_map/ppermute | solution.py:31
  10.8 26.8 %collective-permute-start.8 = (s32[2]{0:T(128)S(1)}, s32[2]{0:T(128)S(1)}, u32[]{:S(2)}, u32[]{:S(2)}) collective-permute-start(s32[2]{0:T(128)S(1)} %get-tuple-element.42), channel_id=1, source_target_pairs={{0,60},{1,61},{2,62},{3,63},{4,0},{5,1},{6,2},{7,3},{8,4},{9,5},{1... | collective-permute-start | bytes 32 | tf_op jit(solution)/shard_map/ppermute | solution.py:31
  12.0 25.6 %collective-permute-start.6 = (s32[2]{0:T(128)S(1)}, s32[2]{0:T(128)S(1)}, u32[]{:S(2)}, u32[]{:S(2)}) collective-permute-start(s32[2]{0:T(128)S(1)} %get-tuple-element.43), channel_id=1, source_target_pairs={{0,61},{1,62},{2,63},{3,0},{4,1},{5,2},{6,3},{7,4},{8,5},{9,6},{10... | collective-permute-start | bytes 32 | tf_op jit(solution)/shard_map/ppermute | solution.py:31
  14.2 23.4 %collective-permute-start.4 = (s32[2]{0:T(128)S(1)}, s32[2]{0:T(128)S(1)}, u32[]{:S(2)}, u32[]{:S(2)}) collective-permute-start(s32[2]{0:T(128)S(1)} %get-tuple-element.44), channel_id=1, source_target_pairs={{0,62},{1,63},{2,0},{3,1},{4,2},{5,3},{6,4},{7,5},{8,6},{9,7},{10,... | collective-permute-start | bytes 32 | tf_op jit(solution)/shard_map/ppermute | solution.py:31
  51.8 56.8 %collective-permute-start.14 = (bf16[2,64,2048]{2,1,0:T(8,128)(2,1)}, bf16[2,64,2048]{2,1,0:T(8,128)(2,1)}, u32[]{:S(2)}, u32[]{:S(2)}) collective-permute-start(bf16[2,64,2048]{2,1,0:T(8,128)(2,1)} %gather_fusion.7), channel_id=1, source_target_pairs={{0,1},{1,2},{2,3},{3,4},{4,5},{5,6},{6,7},{7,8},{8,9},{9,10},{10,1... | collective-permute-start | bytes 1572872 | tf_op jit(solution)/shard_map/ppermute | solution.py:31
  53.2 56.7 %collective-permute-start.3 = (bf16[2,64,2048]{2,1,0:T(8,128)(2,1)}, bf16[2,64,2048]{2,1,0:T(8,128)(2,1)}, u32[]{:S(2)}, u32[]{:S(2)}) collective-permute-start(bf16[2,64,2048]{2,1,0:T(8,128)(2,1)} %gather_fusion), channel_id=1, source_target_pairs={{0,1},{1,2},{2,3},{3,4},{4,5},{5,6},{6,7},{7,8},{8,9},{9,10},{10,1... | collective-permute-start | bytes 1572872 | tf_op jit(solution)/shard_map/ppermute | solution.py:31
  101.4 118.7 %collective-permute-start.5 = (bf16[2,64,2048]{2,1,0:T(8,128)(2,1)}, bf16[2,64,2048]{2,1,0:T(8,128)(2,1)S(1)}, u32[]{:S(2)}, u32[]{:S(2)}) collective-permute-start(bf16[2,64,2048]{2,1,0:T(8,128)(2,1)} %gather_fusion.1), channel_id=1, source_target_pairs={{0,2},{1,3},{2,4},{3,5},{4,6},{5,7},{6,8},{7,9},{8,10},{9,11},{10,... | collective-permute-start | bytes 1572872 | tf_op jit(solution)/shard_map/ppermute | solution.py:31
  101.4 26.3 %collective-permute-start.15 = (bf16[2,64,2048]{2,1,0:T(8,128)(2,1)}, bf16[2,64,2048]{2,1,0:T(8,128)(2,1)}, u32[]{:S(2)}, u32[]{:S(2)}) collective-permute-start(bf16[2,64,2048]{2,1,0:T(8,128)(2,1)} %gather_fusion.8), channel_id=1, source_target_pairs={{0,2},{1,3},{2,4},{3,5},{4,6},{5,7},{6,8},{7,9},{8,10},{9,11},{10,... | collective-permute-start | bytes 1572872 | tf_op jit(solution)/shard_map/ppermute | solution.py:31
  106.0 114.3 %collective-permute-start.7 = (bf16[2,64,2048]{2,1,0:T(8,128)(2,1)}, bf16[2,64,2048]{2,1,0:T(8,128)(2,1)S(1)}, u32[]{:S(2)}, u32[]{:S(2)}) collective-permute-start(bf16[2,64,2048]{2,1,0:T(8,128)(2,1)} %gather_fusion.2), channel_id=1, source_target_pairs={{0,3},{1,4},{2,5},{3,6},{4,7},{5,8},{6,9},{7,10},{8,11},{9,12},{10... | collective-permute-start | bytes 1572872 | tf_op jit(solution)/shard_map/ppermute | solution.py:31
  108.6 60.4 %collective-permute-start.16 = (bf16[2,64,2048]{2,1,0:T(8,128)(2,1)}, bf16[2,64,2048]{2,1,0:T(8,128)(2,1)S(1)}, u32[]{:S(2)}, u32[]{:S(2)}) collective-permute-start(bf16[2,64,2048]{2,1,0:T(8,128)(2,1)} %gather_fusion.9), channel_id=1, source_target_pairs={{0,3},{1,4},{2,5},{3,6},{4,7},{5,8},{6,9},{7,10},{8,11},{9,12},{10... | collective-permute-start | bytes 1572872 | tf_op jit(solution)/shard_map/ppermute | solution.py:31
  109.9 110.4 %collective-permute-start.9 = (bf16[2,64,2048]{2,1,0:T(8,128)(2,1)S(1)}, bf16[2,64,2048]{2,1,0:T(8,128)(2,1)S(1)}, u32[]{:S(2)}, u32[]{:S(2)}) collective-permute-start(bf16[2,64,2048]{2,1,0:T(8,128)(2,1)S(1)} %copy-done.29), channel_id=1, source_target_pairs={{0,4},{1,5},{2,6},{3,7},{4,8},{5,9},{6,10},{7,11},{8,12},{9,13},{1... | collective-permute-start | bytes 1572872 | tf_op jit(solution)/shard_map/ppermute | solution.py:31
  127.8 71.2 %collective-permute-start.17 = (bf16[2,64,2048]{2,1,0:T(8,128)(2,1)}, bf16[2,64,2048]{2,1,0:T(8,128)(2,1)S(1)}, u32[]{:S(2)}, u32[]{:S(2)}) collective-permute-start(bf16[2,64,2048]{2,1,0:T(8,128)(2,1)} %gather_fusion.10), channel_id=1, source_target_pairs={{0,4},{1,5},{2,6},{3,7},{4,8},{5,9},{6,10},{7,11},{8,12},{9,13},{1... | collective-permute-start | bytes 1572872 | tf_op jit(solution)/shard_map/ppermute | solution.py:31
  169.0 30.0 %collective-permute-start.18 = (bf16[2,64,2048]{2,1,0:T(8,128)(2,1)S(1)}, bf16[2,64,2048]{2,1,0:T(8,128)(2,1)S(1)}, u32[]{:S(2)}, u32[]{:S(2)}) collective-permute-start(bf16[2,64,2048]{2,1,0:T(8,128)(2,1)S(1)} %copy-done.31), channel_id=1, source_target_pairs={{0,5},{1,6},{2,7},{3,8},{4,9},{5,10},{6,11},{7,12},{8,13},{9,14},{... | collective-permute-start | bytes 1572872 | tf_op jit(solution)/shard_map/ppermute | solution.py:31
  198.9 21.0 %collective-permute-start.19 = (bf16[2,64,2048]{2,1,0:T(8,128)(2,1)S(1)}, bf16[2,64,2048]{2,1,0:T(8,128)(2,1)S(1)}, u32[]{:S(2)}, u32[]{:S(2)}) collective-permute-start(bf16[2,64,2048]{2,1,0:T(8,128)(2,1)S(1)} %copy-done.30), channel_id=1, source_target_pairs={{0,6},{1,7},{2,8},{3,9},{4,10},{5,11},{6,12},{7,13},{8,14},{9,15},... | collective-permute-start | bytes 1572872 | tf_op jit(solution)/shard_map/ppermute | solution.py:31
  199.0 39.0 %collective-permute-start.11 = (bf16[2,64,2048]{2,1,0:T(8,128)(2,1)S(1)}, bf16[2,64,2048]{2,1,0:T(8,128)(2,1)S(1)}, u32[]{:S(2)}, u32[]{:S(2)}) collective-permute-start(bf16[2,64,2048]{2,1,0:T(8,128)(2,1)S(1)} %copy-done.28), channel_id=1, source_target_pairs={{0,5},{1,6},{2,7},{3,8},{4,9},{5,10},{6,11},{7,12},{8,13},{9,14},{... | collective-permute-start | bytes 1572872 | tf_op jit(solution)/shard_map/ppermute | solution.py:31
  219.9 22.1 %collective-permute-start.13 = (bf16[2,64,2048]{2,1,0:T(8,128)(2,1)S(1)}, bf16[2,64,2048]{2,1,0:T(8,128)(2,1)S(1)}, u32[]{:S(2)}, u32[]{:S(2)}) collective-permute-start(bf16[2,64,2048]{2,1,0:T(8,128)(2,1)S(1)} %copy-done.27), channel_id=1, source_target_pairs={{0,6},{1,7},{2,8},{3,9},{4,10},{5,11},{6,12},{7,13},{8,14},{9,15},... | collective-permute-start | bytes 1572872 | tf_op jit(solution)/shard_map/ppermute | solution.py:31
  299.9 67.3 %collective-permute-start.26 = (bf16[2,131072]{1,0:T(2,128)(2,1)}, bf16[2,131072]{1,0:T(2,128)(2,1)}, u32[]{:S(2)}, u32[]{:S(2)}) collective-permute-start(bf16[2,131072]{1,0:T(2,128)(2,1)} %convert_element_type.110), channel_id=1, source_target_pairs={{0,63},{1,0},{2,1},{3,2},{4,3},{5,4},{6,5},{7,6},{8,7},{9,8},{10,9... | collective-permute-start | bytes 1572872 | tf_op jit(solution)/shard_map/ppermute | solution.py:31
  333.5 36.6 %collective-permute-start.20 = (bf16[2,131072]{1,0:T(2,128)(2,1)}, bf16[2,131072]{1,0:T(2,128)(2,1)}, u32[]{:S(2)}, u32[]{:S(2)}) collective-permute-start(bf16[2,131072]{1,0:T(2,128)(2,1)} %convert_element_type.104), channel_id=1, source_target_pairs={{0,63},{1,0},{2,1},{3,2},{4,3},{5,4},{6,5},{7,6},{8,7},{9,8},{10,9... | collective-permute-start | bytes 1572872 | tf_op jit(solution)/shard_map/ppermute | solution.py:31
  333.5 130.8 %collective-permute-start.21 = (bf16[2,131072]{1,0:T(2,128)(2,1)}, bf16[2,131072]{1,0:T(2,128)(2,1)}, u32[]{:S(2)}, u32[]{:S(2)}) collective-permute-start(bf16[2,131072]{1,0:T(2,128)(2,1)} %convert_element_type.105), channel_id=1, source_target_pairs={{0,62},{1,63},{2,0},{3,1},{4,2},{5,3},{6,4},{7,5},{8,6},{9,7},{10,... | collective-permute-start | bytes 1572872 | tf_op jit(solution)/shard_map/ppermute | solution.py:31
  336.3 138.4 %collective-permute-start.22 = (bf16[2,131072]{1,0:T(2,128)(2,1)}, bf16[2,131072]{1,0:T(2,128)(2,1)}, u32[]{:S(2)}, u32[]{:S(2)}) collective-permute-start(bf16[2,131072]{1,0:T(2,128)(2,1)} %convert_element_type.106), channel_id=1, source_target_pairs={{0,61},{1,62},{2,63},{3,0},{4,1},{5,2},{6,3},{7,4},{8,5},{9,6},{10... | collective-permute-start | bytes 1572872 | tf_op jit(solution)/shard_map/ppermute | solution.py:31
  342.7 134.2 %collective-permute-start.23 = (bf16[2,131072]{1,0:T(2,128)(2,1)}, bf16[2,131072]{1,0:T(2,128)(2,1)}, u32[]{:S(2)}, u32[]{:S(2)}) collective-permute-start(bf16[2,131072]{1,0:T(2,128)(2,1)} %convert_element_type.107), channel_id=1, source_target_pairs={{0,60},{1,61},{2,62},{3,63},{4,0},{5,1},{6,2},{7,3},{8,4},{9,5},{1... | collective-permute-start | bytes 1572872 | tf_op jit(solution)/shard_map/ppermute | solution.py:31
  367.1 112.0 %collective-permute-start.24 = (bf16[2,131072]{1,0:T(2,128)(2,1)}, bf16[2,131072]{1,0:T(2,128)(2,1)S(1)}, u32[]{:S(2)}, u32[]{:S(2)}) collective-permute-start(bf16[2,131072]{1,0:T(2,128)(2,1)} %convert_element_type.108), channel_id=1, source_target_pairs={{0,59},{1,60},{2,61},{3,62},{4,63},{5,0},{6,1},{7,2},{8,3},{9,4},{... | collective-permute-start | bytes 1572872 | tf_op jit(solution)/shard_map/ppermute | solution.py:31
  370.1 27.1 %collective-permute-start.27 = (bf16[2,131072]{1,0:T(2,128)(2,1)}, bf16[2,131072]{1,0:T(2,128)(2,1)S(1)}, u32[]{:S(2)}, u32[]{:S(2)}) collective-permute-start(bf16[2,131072]{1,0:T(2,128)(2,1)} %convert_element_type.111), channel_id=1, source_target_pairs={{0,62},{1,63},{2,0},{3,1},{4,2},{5,3},{6,4},{7,5},{8,6},{9,7},{10,... | collective-permute-start | bytes 1572872 | tf_op jit(solution)/shard_map/ppermute | solution.py:31
  397.2 28.1 %collective-permute-start.28 = (bf16[2,131072]{1,0:T(2,128)(2,1)}, bf16[2,131072]{1,0:T(2,128)(2,1)S(1)}, u32[]{:S(2)}, u32[]{:S(2)}) collective-permute-start(bf16[2,131072]{1,0:T(2,128)(2,1)} %convert_element_type.112), channel_id=1, source_target_pairs={{0,61},{1,62},{2,63},{3,0},{4,1},{5,2},{6,3},{7,4},{8,5},{9,6},{10... | collective-permute-start | bytes 1572872 | tf_op jit(solution)/shard_map/ppermute | solution.py:31
  425.3 26.8 %collective-permute-start.29 = (bf16[2,131072]{1,0:T(2,128)(2,1)S(1)}, bf16[2,131072]{1,0:T(2,128)(2,1)S(1)}, u32[]{:S(2)}, u32[]{:S(2)}) collective-permute-start(bf16[2,131072]{1,0:T(2,128)(2,1)S(1)} %copy-done.26), channel_id=1, source_target_pairs={{0,60},{1,61},{2,62},{3,63},{4,0},{5,1},{6,2},{7,3},{8,4},{9,5},{1... | collective-permute-start | bytes 1572872 | tf_op jit(solution)/shard_map/ppermute | solution.py:31
  452.1 10.7 %collective-permute-start.30 = (bf16[2,131072]{1,0:T(2,128)(2,1)S(1)}, bf16[2,131072]{1,0:T(2,128)(2,1)S(1)}, u32[]{:S(2)}, u32[]{:S(2)}) collective-permute-start(bf16[2,131072]{1,0:T(2,128)(2,1)S(1)} %copy-done.25), channel_id=1, source_target_pairs={{0,59},{1,60},{2,61},{3,62},{4,63},{5,0},{6,1},{7,2},{8,3},{9,4},{... | collective-permute-start | bytes 1572872 | tf_op jit(solution)/shard_map/ppermute | solution.py:31
  462.8 32.1 %collective-permute-start.25 = (bf16[2,131072]{1,0:T(2,128)(2,1)S(1)}, bf16[2,131072]{1,0:T(2,128)(2,1)S(1)}, u32[]{:S(2)}, u32[]{:S(2)}) collective-permute-start(bf16[2,131072]{1,0:T(2,128)(2,1)S(1)} %copy-done.23), channel_id=1, source_target_pairs={{0,58},{1,59},{2,60},{3,61},{4,62},{5,63},{6,0},{7,1},{8,2},{9,3},... | collective-permute-start | bytes 1572872 | tf_op jit(solution)/shard_map/ppermute | solution.py:31
  464.3 40.7 %collective-permute-start.31 = (bf16[2,131072]{1,0:T(2,128)(2,1)S(1)}, bf16[2,131072]{1,0:T(2,128)(2,1)}, u32[]{:S(2)}, u32[]{:S(2)}) collective-permute-start(bf16[2,131072]{1,0:T(2,128)(2,1)S(1)} %copy-done.24), channel_id=1, source_target_pairs={{0,58},{1,59},{2,60},{3,61},{4,62},{5,63},{6,0},{7,1},{8,2},{9,3},... | collective-permute-start | bytes 1572872 | tf_op jit(solution)/shard_map/ppermute | solution.py:31
  670.0 7.8 %collective-permute-start.37 = (f32[3,4,2048]{2,0,1:T(4,128)S(1)}, f32[3,4,2048]{2,0,1:T(4,128)S(1)}, u32[]{:S(2)}, u32[]{:S(2)}) collective-permute-start(f32[3,4,2048]{2,0,1:T(4,128)S(1)} %add.762), channel_id=1, source_target_pairs={{0,8},{1,9},{2,10},{3,11},{4,12},{5,13},{6,14},{7,15},{8,0},{9,1},... | collective-permute-start | bytes 294920 | tf_op jit(solution)/shard_map/ppermute | solution.py:38
  677.9 8.8 %collective-permute-start.38 = (f32[3,4,2048]{2,0,1:T(4,128)S(1)}, f32[3,4,2048]{2,0,1:T(4,128)S(1)}, u32[]{:S(2)}, u32[]{:S(2)}) collective-permute-start(f32[3,4,2048]{2,0,1:T(4,128)S(1)} %add.763), channel_id=1, source_target_pairs={{0,16},{1,17},{2,18},{3,19},{4,20},{5,21},{6,22},{7,23},{8,24},{9,... | collective-permute-start | bytes 294920 | tf_op jit(solution)/shard_map/ppermute | solution.py:38
  686.7 10.3 %collective-permute-start.39 = (f32[3,4,2048]{2,0,1:T(4,128)S(1)}, f32[3,4,2048]{2,0,1:T(4,128)S(1)}, u32[]{:S(2)}, u32[]{:S(2)}) collective-permute-start(f32[3,4,2048]{2,0,1:T(4,128)S(1)} %add.764), channel_id=1, source_target_pairs={{0,32},{1,33},{2,34},{3,35},{4,36},{5,37},{6,38},{7,39},{8,40},{9,... | collective-permute-start | bytes 294920 | tf_op jit(solution)/shard_map/ppermute | solution.py:38
  (58 other events, 1342.7 us)
